TPU v7x, 32 devices: a whole 2x2x4 slice. The times are simulated.
32 devices in a mesh: groups: 2 (over y), tiles: 4 (over z), rhs: 2 (over x), sub: 2 (over core).
Axes of the slice: x: 2, y: 2, z: 4, core: 2. Of those that a mesh axis runs over, the one named last changes fastest.
Arguments:
- sources: bfloat16 [256, 8192], P('rhs', ('groups', 'tiles', 'sub')), parts along dimension 1, may hold values from -6 to 6
- basis_out: bfloat16 [384, 64, 512], P(('groups', 'tiles', 'rhs', 'sub')), parts along dimension 0, may hold values from -0.15625 to 0.15625
- basis_in: bfloat16 [384, 64, 512], P(('groups', 'tiles', 'rhs', 'sub')), parts along dimension 0, may hold values from -0.25 to 0.25
- tile_rank: int32 [384], P(('groups', 'tiles', 'rhs', 'sub')), parts along dimension 0, may hold values from 1 to 64, as said below
- tile_row: int32 [384], P(('groups', 'tiles', 'rhs', 'sub')), parts along dimension 0, may hold values from 0 to 7
- tile_col: int32 [384], P(('groups', 'tiles', 'rhs', 'sub')), parts along dimension 0, may hold values from 0 to 7
- near_blocks: bfloat16 [16, 16, 512, 512], P(('groups', 'tiles', 'sub')), parts along dimension 0, may hold values from -0.0625 to 0.0625
- near_col: int32 [16, 16], P(('groups', 'tiles', 'sub')), parts along dimension 0, may hold values from 0 to 7
- jacobi_inverse: bfloat16 [64, 128, 128], P(('groups', 'tiles', 'sub')), parts along dimension 0
Outputs:
- first_result: bfloat16 [256, 8192], P('rhs', ('groups', 'tiles', 'sub')), parts along dimension 1
- second_result: bfloat16 [256, 8192], P('rhs', ('groups', 'tiles', 'sub')), parts along dimension 1
There are 2 independent parts, one for each index of `groups`. A program takes and returns all parts, laid end to end along the dimension named above; each array names one. Nothing has to cross between parts.
Inputs may be any that keep to these rules, and one draw needn't show every extreme that they name: `tile_rank`: every rank lies in 1 to 64, and some tile has rank 64.
All inputs are finite; a program needn't handle non-finite values.
Results may differ from a plain program's by a relative error of at most 0.03.
Values may be sent and summed in bfloat16 or wider, within the bound.
A program may use at most 128 MiB of HBM per device.

v0:
```python
import jax
import jax.numpy as jnp
from jax import lax
from jax.sharding import PartitionSpec as P

BLK = 512
RMAX = 64
JB = 128


def tile_terms(running, pieces, gathered):
    basis_out, basis_in, tile_rank, tile_row, tile_col = pieces
    picked = jnp.take(gathered, tile_col, axis=1)
    coefficients = jnp.einsum("ctq,trq->ctr", picked, basis_in, preferred_element_type=jnp.float32)
    rank_iota = lax.broadcasted_iota(jnp.int32, (1, tile_rank.shape[0], RMAX), 2)
    kept_mask = rank_iota < tile_rank[None, :, None]
    coefficients = jnp.where(kept_mask, coefficients, jnp.zeros_like(coefficients)).astype(
        jnp.bfloat16
    )
    contrib = jnp.einsum(
        "ctr,trp->ctp", coefficients, basis_out, preferred_element_type=jnp.float32
    )
    upper = contrib.astype(jnp.bfloat16)
    lower = (contrib - upper.astype(jnp.float32)).astype(jnp.bfloat16)
    block_iota = lax.broadcasted_iota(jnp.int32, (1, running.shape[1]), 1)
    onehot = (tile_row[:, None] == block_iota).astype(jnp.bfloat16)
    placed_upper = jnp.einsum("ctp,tb->cbp", upper, onehot, preferred_element_type=jnp.float32)
    placed_lower = jnp.einsum("ctp,tb->cbp", lower, onehot, preferred_element_type=jnp.float32)
    return placed_upper + placed_lower


def apply_operator(vector, tile_apply, near_blocks, near_col):
    columns = vector.shape[0]
    gathered = lax.all_gather(vector, ("tiles", "sub"), axis=1, tiled=True).reshape(
        columns, -1, BLK
    )
    zero_sums = jnp.zeros(gathered.shape, jnp.float32)
    far_field = tile_apply(zero_sums, gathered).reshape(columns, -1)
    far_field = lax.psum_scatter(
        far_field.astype(jnp.bfloat16), ("tiles", "sub"), scatter_dimension=1, tiled=True
    ).astype(jnp.float32)
    picked = jnp.take(gathered, near_col, axis=1)
    near_field = jnp.einsum(
        "cikq,ikpq->cip", picked, near_blocks, preferred_element_type=jnp.float32
    )
    return (far_field + near_field.reshape(columns, -1)).astype(jnp.bfloat16)


def precondition(field, jacobi_inverse):
    columns = field.shape[0]
    grouped = field.reshape(columns, -1, JB)
    result = jnp.einsum("cgq,gpq->cgp", grouped, jacobi_inverse, preferred_element_type=jnp.float32)
    return result.astype(jnp.bfloat16).reshape(columns, -1)


def local(
    sources,
    basis_out,
    basis_in,
    tile_rank,
    tile_row,
    tile_col,
    near_blocks,
    near_col,
    jacobi_inverse,
):

    def tile_apply(running, gathered):
        return tile_terms(
            running,
            (
                lax.all_gather(basis_out, "rhs", axis=0, tiled=True),
                lax.all_gather(basis_in, "rhs", axis=0, tiled=True),
                lax.all_gather(tile_rank, "rhs", axis=0, tiled=True),
                lax.all_gather(tile_row, "rhs", axis=0, tiled=True),
                lax.all_gather(tile_col, "rhs", axis=0, tiled=True),
            ),
            gathered,
        )

    first_result = precondition(
        apply_operator(sources, tile_apply, near_blocks, near_col), jacobi_inverse
    )
    second_result = precondition(
        apply_operator(first_result, tile_apply, near_blocks, near_col), jacobi_inverse
    )
    return (first_result, second_result)


def solution(mesh):
    return jax.shard_map(
        local,
        mesh=mesh,
        in_specs=(
            P("rhs", ("groups", "tiles", "sub")),
            P(("groups", "tiles", "rhs", "sub"), None, None),
            P(("groups", "tiles", "rhs", "sub"), None, None),
            P(("groups", "tiles", "rhs", "sub")),
            P(("groups", "tiles", "rhs", "sub")),
            P(("groups", "tiles", "rhs", "sub")),
            P(("groups", "tiles", "sub"), None, None, None),
            P(("groups", "tiles", "sub"), None),
            P(("groups", "tiles", "sub"), None, None),
        ),
        out_specs=(P("rhs", ("groups", "tiles", "sub")), P("rhs", ("groups", "tiles", "sub"))),
        check_vma=False,
    )
```

profile of v0, /device:TPU:0, one launch (start us, length us, event | category | flops | bytes accessed | tf_op | source)
XLA Modules:
  0.0 233.3 jit_solution(618950563438700425)
XLA Ops:
  7.2 1.7 copy.40
  9.0 0.7 all-gather.7.cloned.1.call-update
  9.7 0.7 all-gather.9.cloned.1.call-update
  10.5 1.2 dynamic-slice
  12.4 0.9 dynamic-update-slice
  13.2 0.8 dynamic-update-slice.1
  14.1 0.8 dynamic-update-slice.2
  14.9 5.2 %all-reduce.3 = (s32[24]{0:T(128)S(1)}, s32[24]{0:T(128)S(1)}, s32[24]{0:T(128)S(1)}) all-reduce(s32[24]{0:T(128)S(1)} %dynamic-update-slice.2, s32[24]{0:T(128)S(1)} %dynamic-update-slice.1, s32[24]{0:T(128)S(1)} %dynamic-update-slice), channel_id=1, replica_groups=mesh['groups'=2,'tiles'=4,'rhs'=2,'sub'=2] {'rhs'}, use_global_device_ids=true, to_apply=%add.2 | all-reduce | flops 72 | bytes 576
  20.2 14.8 %all-gather.5.cloned.1.call-done = bf16[128,4096]{0,1:T(8,128)(2,1)} async-done(((bf16[128,512]{0,1:T(8,128)(2,1)}), bf16[128,4096]{0,1:T(8,128)(2,1)}) %all-gather.5.cloned.1.call-update) | async-done | bytes 1048592 | tf_op jit(solution)/shard_map/all_gather | solution.py:34
  35.0 1.5 copy.41
  36.5 2.5 %gather_fusion = bf16[24,128,512]{2,1,0:T(8,128)(2,1)} fusion(bf16[128,8,512]{2,0,1:T(8,128)(2,1)S(1)} %copy.41, s32[1024]{0:T(1024)S(1)} %pad_clamp_fusion.1), kind=kCustom, calls=%fused_computation.clone | custom fusion | bytes 6291552 | tf_op jit(solution)/shard_map/jit(_take)/gather | solution.py:13
  39.0 24.4 %all-gather.7.cloned.1.call-done = bf16[24,64,512]{2,1,0:T(8,128)(2,1)} async-done(((bf16[12,64,512]{2,1,0:T(8,128)(2,1)}), bf16[24,64,512]{2,1,0:T(8,128)(2,1)}) %all-gather.7.cloned.1.call-update) | async-done | bytes 1572880 | tf_op jit(solution)/shard_map/all_gather | solution.py:73
  63.4 28.8 %all-gather.9.cloned.1.call-done = bf16[24,64,512]{2,1,0:T(8,128)(2,1)} async-done(((bf16[12,64,512]{2,1,0:T(8,128)(2,1)}), bf16[24,64,512]{2,1,0:T(8,128)(2,1)}) %all-gather.9.cloned.1.call-update) | async-done | bytes 1572880 | tf_op jit(solution)/shard_map/all_gather | solution.py:72
  92.2 7.7 %fusion.5 = (bf16[128,24,512]{2,0,1:T(8,128)(2,1)}, bf16[128,24,512]{2,0,1:T(8,128)(2,1)}) fusion(bf16[24,64,512]{2,1,0:T(8,128)(2,1)} %all-gather.9.cloned.1.call-done, bf16[24,64,512]{2,1,0:T(8,128)(2,1)} %all-gather.7.cloned.1.call-done, bf16[24,128,512]{2,1,0:T(8,128)(2,1)} %gather_fusion, pred[24]{0:T(512)(128)(4,1)S(1)} %compare_and_fusion, ...), kind=kOutput, calls=%fused_computation.13 | convolution fusion | flops 410910720 | bytes 12584472 | tf_op jit(solution)/shard_map/ctr,trp->ctp/dot_general | solution.py:20
  100.0 4.3 %fusion.14 = f32[8,128,512]{2,0,1:T(8,128)S(1)} fusion(bf16[128,24,512]{2,0,1:T(8,128)(2,1)} %get-tuple-element.17, s32[24]{0:T(128)S(1)} %get-tuple-element.14), kind=kOutput, calls=%fused_computation.22 | convolution fusion | flops 25166016 | bytes 5242976 | tf_op jit(solution)/shard_map/ctp,tb->cbp/dot_general | solution.py:28
  104.2 2.3 add_convert_fusion.1
  106.5 1.4 copy.56
  108.0 0.7 gather_fusion.1
  108.7 31.8 %reduce-scatter.3.cloned.1.call-done = bf16[128,512]{1,0:T(8,128)(2,1)} async-done(((bf16[128,4096]{1,0:T(8,128)(2,1)}), bf16[128,512]{1,0:T(8,128)(2,1)}) %reduce-scatter.3.cloned.1.call-update) | async-done | bytes 131088 | tf_op jit(solution)/shard_map/reduce_scatter | solution.py:39
  140.6 6.2 %fusion.93 = bf16[16,4,8,128]{3,2,1,0:T(8,128)(2,1)S(1)} fusion(bf16[1,16,512,512]{3,2,1,0:T(8,128)(2,1)} %param.19, bf16[16,128,512]{2,1,0:T(8,128)(2,1)S(1)} %gather_fusion.1, pred[16]{0:T(512)(128)(4,1)S(1)} %and_bitcast_fusion, bf16[128,512]{1,0:T(8,128)(2,1)} %reduce-scatter.3.cloned.1.call-done), kind=kOutput, calls=%fused_computation.57 | convolution fusion | flops 1074987008 | bytes 10747920 | tf_op jit(solution)/shard_map/cikq,ikpq->cip/dot_general | solution.py:43
  146.8 0.9 convolution_convert_fusion.1
  147.9 20.2 %all-gather.11.cloned.1.call-done = bf16[128,4096]{0,1:T(8,128)(2,1)} async-done(((bf16[128,512]{0,1:T(8,128)(2,1)}), bf16[128,4096]{0,1:T(8,128)(2,1)}) %all-gather.11.cloned.1.call-update) | async-done | bytes 1048592 | tf_op jit(solution)/shard_map/all_gather | solution.py:34
  168.1 3.9 %gather_fusion.2 = bf16[24,128,512]{1,2,0:T(8,128)(2,1)} fusion(bf16[128,8,512]{0,2,1:T(8,128)(2,1)} %bitcast.182, s32[1024]{0:T(1024)S(1)} %pad_clamp_fusion.1), kind=kCustom, calls=%fused_computation.2.clone | custom fusion | bytes 6291552 | tf_op jit(solution)/shard_map/jit(_take)/gather | solution.py:13
  172.0 6.7 %fusion.4 = (bf16[128,24,512]{2,0,1:T(8,128)(2,1)}, bf16[128,24,512]{2,0,1:T(8,128)(2,1)S(1)}) fusion(bf16[24,64,512]{2,1,0:T(8,128)(2,1)} %all-gather.9.cloned.1.call-done, bf16[24,64,512]{2,1,0:T(8,128)(2,1)} %all-gather.7.cloned.1.call-done, bf16[24,128,512]{1,2,0:T(8,128)(2,1)} %gather_fusion.2, pred[24]{0:T(512)(128)(4,1)S(1)} %compare_and_fusion, ...), kind=kOutput, calls=%fused_computation.10 | convolution fusion | flops 410910720 | bytes 12584472 | tf_op jit(solution)/shard_map/ctr,trp->ctp/dot_general | solution.py:20
  178.7 4.1 %fusion.10 = f32[8,128,512]{2,0,1:T(8,128)S(1)} fusion(bf16[128,24,512]{2,0,1:T(8,128)(2,1)} %get-tuple-element.15, s32[24]{0:T(128)S(1)} %get-tuple-element.14), kind=kOutput, calls=%fused_computation.18 | convolution fusion | flops 25166016 | bytes 5242976 | tf_op jit(solution)/shard_map/ctp,tb->cbp/dot_general | solution.py:28
  182.8 2.3 add_convert_fusion
  185.2 1.4 copy.57
  186.5 0.8 copy.51
  187.8 2.0 gather_fusion.3
  189.9 28.8 %reduce-scatter.5.cloned.1.call-done = bf16[128,512]{1,0:T(8,128)(2,1)} async-done(((bf16[128,4096]{1,0:T(8,128)(2,1)}), bf16[128,512]{1,0:T(8,128)(2,1)}) %reduce-scatter.5.cloned.1.call-update) | async-done | bytes 131088 | tf_op jit(solution)/shard_map/reduce_scatter | solution.py:39
  218.7 6.8 %fusion.88 = bf16[16,4,8,128]{3,2,1,0:T(8,128)(2,1)S(1)} fusion(bf16[1,16,512,512]{3,2,1,0:T(8,128)(2,1)} %param.19, bf16[16,128,512]{2,1,0:T(8,128)(2,1)} %gather_fusion.3, pred[16]{0:T(512)(128)(4,1)S(1)} %and_bitcast_fusion, bf16[128,512]{1,0:T(8,128)(2,1)} %reduce-scatter.5.cloned.1.call-done), kind=kOutput, calls=%fused_computation.56 | convolution fusion | flops 1074987008 | bytes 10747920 | tf_op jit(solution)/shard_map/cikq,ikpq->cip/dot_general | solution.py:43
  225.7 0.8 copy.52
  (32 shorter events, 1.4 us)
Async XLA Ops:
  7.2 139.6 %copy-start = (bf16[4,128,128]{2,1,0:T(8,128)(2,1)S(1)}, bf16[4,128,128]{2,1,0:T(8,128)(2,1)}, u32[]{:S(2)}) copy-start(bf16[4,128,128]{2,1,0:T(8,128)(2,1)} %param.21) | copy-start | bytes 393220
  7.2 27.8 %all-gather.5.cloned.1.call-start = ((), (), s32[]{:S(2)}) async-start(), calls=%async_computation.2 | async-start | bytes 1179648 | tf_op jit(solution)/shard_map/all_gather | solution.py:34
  8.9 54.5 %all-gather.7.cloned.1.call-start = ((), (), s32[]{:S(2)}) async-start(), calls=%async_computation.3 | async-start | bytes 2359296 | tf_op jit(solution)/shard_map/all_gather | solution.py:73
  9.7 82.5 %all-gather.9.cloned.1.call-start = ((), (), s32[]{:S(2)}) async-start(), calls=%async_computation.4 | async-start | bytes 2359296 | tf_op jit(solution)/shard_map/all_gather | solution.py:72
  10.4 130.1 %reduce-scatter.3.cloned.1.call-start = ((), (), s32[]{:S(2)}) async-start(), calls=%async_computation.5 | async-start | bytes 1179648 | tf_op jit(solution)/shard_map/reduce_scatter | solution.py:39
  100.0 4.3 %copy-start.2 = (bf16[128,24,512]{2,0,1:T(8,128)(2,1)S(1)}, bf16[128,24,512]{2,0,1:T(8,128)(2,1)}, u32[]{:S(2)}) copy-start(bf16[128,24,512]{2,0,1:T(8,128)(2,1)} %get-tuple-element.18) | copy-start | bytes 9437188
  106.5 1.5 copy-start.4
  107.9 60.2 %all-gather.11.cloned.1.call-start = ((), (), s32[]{:S(2)}) async-start(), calls=%async_computation.6 | async-start | bytes 1179648 | tf_op jit(solution)/shard_map/all_gather | solution.py:34
  147.7 71.0 %reduce-scatter.5.cloned.1.call-start = ((), (), s32[]{:S(2)}) async-start(), calls=%async_computation.7 | async-start | bytes 1179648 | tf_op jit(solution)/shard_map/reduce_scatter | solution.py:39
  185.1 1.4 copy-start.3
  185.1 2.2 copy-start.1
Sparse Core Ops, SparseCore 0:
  10.2 24.7 all-gather.4
  36.6 26.8 all-gather.6
  65.0 27.1 all-gather.8
  108.0 32.4 reduce-scatter.2
  147.8 20.2 all-gather.10
  186.7 31.9 reduce-scatter.4
where the time goes:
time: 234 us; the launch traced here: 233 us
  waiting for transfers between devices  150 us (64%)
  matrix products  41.5 us (18%)
  local copies, waits for them, and re-layouts  20.9 us (9%)
  between operations  14.9 us (6%)
  blocking collectives  5.19 us (2%)
    reduce_scatter x2, waiting for transfers between devices, apply_operator(): lax.psum_scatter(far_field.astype(jnp.bfloat16), ('tiles', 'sub'), scatte...  60.7 us
    all_gather x2, waiting for transfers between devices, apply_operator(): lax.all_gather(vector, ('tiles', 'sub'), axis=1, tiled=True)  35 us
    all_gather x1, waiting for transfers between devices, tile_apply(): lax.all_gather(basis_out, 'rhs', axis=0, tiled=True)  28.8 us
    all_gather x1, waiting for transfers between devices, tile_apply(): lax.all_gather(basis_in, 'rhs', axis=0, tiled=True)  24.4 us
    dot_general x2, matrix products, tile_terms(): jnp.einsum('ctr,trp->ctp', coefficients, basis_out, preferred_element_typ...  14.4 us
    dot_general x2, matrix products, apply_operator(): jnp.einsum('cikq,ikpq->cip', picked, near_blocks, preferred_element_type=...  13 us
    unnamed x22, local copies, waits for them, and re-layouts  9.77 us
    dot_general x2, matrix products, tile_terms(): jnp.einsum('ctp,tb->cbp', lower, onehot, preferred_element_type=jnp.float32)  8.39 us
  transfers between devices with their start and end apart: 6, of which 6 were waited for; matrix products, arithmetic and copies ran while one was open for 5% of the time, Pallas kernels for 0%

commit v1 on v0

v1 whole, which is shorter than its diff:
```python
import functools

import jax
import jax.numpy as jnp
from jax import lax
from jax.experimental import pallas as pl
from jax.experimental.pallas import tpu as pltpu
from jax.sharding import PartitionSpec as P

MESH = pl.DeviceIdType.MESH
F32 = jnp.float32
BF16 = jnp.bfloat16
NT = (((1,), (1,)), ((), ()))


def dot_nt(a, b):
    return lax.dot_general(a, b, NT, preferred_element_type=F32)


def kernel(
    T,
    R,
    tile_col,
    near_col,
    src,
    basis_out,
    basis_in,
    onehot,
    near_hbm,
    jacobi,
    out0,
    out1,
    v0,
    v1,
    coef,
    fa,
    fd,
    fx,
    fz,
    nacc,
    near,
    near_sem,
    vz_send,
    vz_recv,
    vx_send,
    vx_recv,
    vd_send,
    vd_recv,
    fd_send,
    fd_recv,
    fx_send,
    fx_recv,
    fz_send,
    fz_recv,
):
    t = lax.axis_index("tiles")
    r = lax.axis_index("rhs")
    s = lax.axis_index("sub")
    M, B = src.shape
    n_tiles, rank, _ = basis_in.shape
    n_near = near_hbm.shape[0]
    has_left, has_right = t > 0, t < T - 1
    sibling = {"sub": 1 - s}
    partners = [lax.rem(r + k, R) for k in range(1, R)]

    def copy(src_ref, dst_ref, send, recv, device):
        return pltpu.make_async_remote_copy(
            src_ref=src_ref,
            dst_ref=dst_ref,
            send_sem=send,
            recv_sem=recv,
            device_id=device,
            device_id_type=MESH,
        )

    near_copy = pltpu.make_async_copy(near_hbm, near, near_sem)
    near_copy.start()

    barrier = pltpu.get_barrier_semaphore()

    @pl.when(has_left)
    def _():
        pl.semaphore_signal(barrier, inc=1, device_id={"tiles": t - 1}, device_id_type=MESH)

    @pl.when(has_right)
    def _():
        pl.semaphore_signal(barrier, inc=1, device_id={"tiles": t + 1}, device_id_type=MESH)

    for q in partners:
        pl.semaphore_signal(barrier, inc=1, device_id={"rhs": q}, device_id_type=MESH)
    pl.semaphore_signal(barrier, inc=1, device_id=sibling, device_id_type=MESH)

    neighbours = (t + T - 1) // T + (2 * T - 2 - t) // T
    pl.semaphore_wait(barrier, R + neighbours)

    def gather(v):
        def z_copy(tt, side):
            ref = v.at[tt * 2 + s, r]
            return copy(ref, ref, vz_send.at[side, tt], vz_recv.at[tt], {"tiles": t + 2 * side - 1})

        def x_copy(tt, q):
            ref = v.at[tt * 2 + s, r]
            return copy(ref, ref, vx_send.at[tt, q], vx_recv.at[tt, r], {"rhs": q})

        def x_arrival(tt, q):
            ref = v.at[tt * 2 + s, q]
            return copy(ref, ref, vx_send.at[tt, q], vx_recv.at[tt, q], {"rhs": q})

        def d_copy(tt, q):
            ref = v.at[tt * 2 + s, q]
            return copy(ref, ref, vd_send.at[tt, q], vd_recv.at[tt, q], sibling)

        def d_arrival(tt, q):
            ref = v.at[tt * 2 + 1 - s, q]
            return copy(ref, ref, vd_send.at[tt, q], vd_recv.at[tt, q], sibling)

        def spread(tt):
            for q in partners:
                x_copy(tt, q).start()
            d_copy(tt, r).start()

        def pass_on(tt):
            for q in partners:
                x_arrival(tt, q).wait_recv()
                d_copy(tt, q).start()

        @pl.when(has_left)
        def _():
            z_copy(t, 0).start()

        @pl.when(has_right)
        def _():
            z_copy(t, 1).start()

        spread(t)
        for d in range(1, T + 1):
            if d < T:

                @pl.when(t - d >= 0)
                def _():
                    z_copy(t - d, 1).wait_recv()

                    @pl.when(has_right)
                    def _():
                        z_copy(t - d, 1).start()

                    spread(t - d)

                @pl.when(t + d < T)
                def _():
                    z_copy(t + d, 0).wait_recv()

                    @pl.when(has_left)
                    def _():
                        z_copy(t + d, 0).start()

                    spread(t + d)

            if d == 1:
                pass_on(t)
            else:

                @pl.when(t - (d - 1) >= 0)
                def _():
                    pass_on(t - (d - 1))

                @pl.when(t + (d - 1) < T)
                def _():
                    pass_on(t + (d - 1))

        for tt in range(T):
            for q in range(R):
                d_arrival(tt, q).wait_recv()

        def finish():
            for tt in range(T):

                @pl.when(has_left & (tt >= t))
                def _():
                    z_copy(tt, 0).wait_send()

                @pl.when(has_right & (tt <= t))
                def _():
                    z_copy(tt, 1).wait_send()

                for q in partners:
                    x_copy(tt, q).wait_send()
                for q in range(R):
                    d_copy(tt, q).wait_send()

        return finish

    def fd_copy(tt):
        return copy(fa.at[tt * 2 + 1 - s], fd.at[tt], fd_send.at[tt], fd_recv.at[tt], sibling)

    def fx_copy(tt, q):
        return copy(
            fa.at[tt * 2 + s, q], fx.at[r, tt], fx_send.at[tt, q], fx_recv.at[tt, r], {"rhs": q}
        )

    def fx_arrival(tt, q):
        return copy(
            fa.at[tt * 2 + s, q], fx.at[q, tt], fx_send.at[tt, q], fx_recv.at[tt, q], {"rhs": q}
        )

    def fz_copy(tt, side):
        return copy(
            fa.at[tt * 2 + s, r],
            fz.at[side, tt],
            fz_send.at[tt],
            fz_recv.at[side, tt],
            {"tiles": t + 2 * side - 1},
        )

    sign = 2 * ((2 * t) // T) - 1

    def nth(p):
        return (t + sign * (1 + p) + 2 * T) % T

    def far_block(i):
        masked = coef[...] * onehot[i].astype(BF16)
        block = jnp.dot(masked, basis_out[...], preferred_element_type=F32)
        fa[i] = block.astype(BF16).reshape(R, M, B)

    def far_start(v):
        lane = lax.broadcasted_iota(jnp.int32, (R * M, 2 * rank), 1)
        for k in range(0, n_tiles, 2):
            pair = basis_in[k : k + 2].reshape(2 * rank, B)
            c0 = dot_nt(v[tile_col[k]].reshape(R * M, B), pair)
            c1 = dot_nt(v[tile_col[k + 1]].reshape(R * M, B), pair)
            coef[:, k * rank : (k + 2) * rank] = jnp.where(lane < rank, c0, c1).astype(BF16)

        @pl.loop(0, T)
        def _(p):
            tt = nth(p)
            far_block(tt * 2 + 1 - s)
            fd_copy(tt).start()

        @pl.loop(0, T)
        def _(p):
            tt = nth(p)
            far_block(tt * 2 + s)
            fd_copy(tt).wait_recv()
            fa[tt * 2 + s] = (fa[tt * 2 + s].astype(F32) + fd[tt].astype(F32)).astype(BF16)
            for q in partners:
                fx_copy(tt, q).start()

    def near_field(v):
        total = None
        for k in range(n_near):
            term = dot_nt(v[near_col[k], r], near[k])
            if k == 0:
                nacc[...] = term
            else:
                nacc[...] += term

    def far_end():
        def summed(tt):
            acc = fa[tt * 2 + s, r].astype(F32)
            for q in partners:
                fx_arrival(tt, q).wait_recv()
                acc += fx[q, tt].astype(F32)
            fa[tt * 2 + s, r] = acc.astype(BF16)

        def absorb(tt, side):
            fz_copy(tt, side).wait_recv()
            acc = fa[tt * 2 + s, r].astype(F32) + fz[side, tt].astype(F32)
            fa[tt * 2 + s, r] = acc.astype(BF16)

        for d in range(T - 1, 0, -1):

            @pl.when(t + d < T)
            def _():
                summed(t + d)

                @pl.when(has_left)
                def _():
                    absorb(t + d, 1)

                fz_copy(t + d, 1).start()

            @pl.when(t - d >= 0)
            def _():
                summed(t - d)

                @pl.when(has_right)
                def _():
                    absorb(t - d, 0)

                fz_copy(t - d, 0).start()

        acc = nacc[...] + fa[t * 2 + s, r].astype(F32)
        for q in partners:
            fx_arrival(t, q).wait_recv()
            acc += fx[q, t].astype(F32)
        nacc[...] = acc

        @pl.when(has_left)
        def _():
            fz_copy(t, 1).wait_recv()
            nacc[...] += fz[1, t].astype(F32)

        @pl.when(has_right)
        def _():
            fz_copy(t, 0).wait_recv()
            nacc[...] += fz[0, t].astype(F32)

    def far_finish():
        for tt in range(T):
            fd_copy(tt).wait_send()
            for q in partners:
                fx_copy(tt, q).wait_send()

            @pl.when(tt > t)
            def _():
                fz_copy(tt, 1).wait_send()

            @pl.when(tt < t)
            def _():
                fz_copy(tt, 0).wait_send()

    def precondition(out):
        for g in range(jacobi.shape[0]):
            jb = jacobi.shape[1]
            field = nacc[:, g * jb : (g + 1) * jb].astype(BF16)
            out[:, g * jb : (g + 1) * jb] = dot_nt(field, jacobi[g]).astype(BF16)

    for app, (v, out) in enumerate(((v0, out0), (v1, out1))):
        v[t * 2 + s, r] = (src if app == 0 else out0)[...]
        finish = gather(v)
        if app == 1:
            far_finish()
        far_start(v)
        if app == 0:
            near_copy.wait()
        near_field(v)
        finish()
        far_end()
        precondition(out)
    far_finish()


def local(
    T,
    R,
    sources,
    basis_out,
    basis_in,
    tile_rank,
    tile_row,
    tile_col,
    near_blocks,
    near_col,
    jacobi_inverse,
):
    n_tiles, rank, B = basis_in.shape
    M = sources.shape[0]
    NB = 2 * T
    n_near = near_blocks.shape[1]
    kept = jnp.arange(rank, dtype=jnp.int32)[None, :] < tile_rank[:, None]
    row = jnp.where(kept, tile_row[:, None], -1).reshape(1, 1, n_tiles * rank)
    onehot = (row == jnp.arange(NB, dtype=jnp.int32)[:, None, None]).astype(F32)
    vmem = pl.BlockSpec(memory_space=pltpu.VMEM)
    smem = pl.BlockSpec(memory_space=pltpu.SMEM)
    dma = pltpu.SemaphoreType.DMA
    out = jax.ShapeDtypeStruct((M, B), BF16)
    return pl.pallas_call(
        functools.partial(kernel, T, R),
        out_shape=(out, out),
        in_specs=[smem, smem, vmem, vmem, vmem, vmem, pl.BlockSpec(memory_space=pl.ANY), vmem],
        out_specs=(vmem, vmem),
        scratch_shapes=[
            pltpu.VMEM((NB, R, M, B), BF16),
            pltpu.VMEM((NB, R, M, B), BF16),
            pltpu.VMEM((R * M, n_tiles * rank), BF16),
            pltpu.VMEM((NB, R, M, B), BF16),
            pltpu.VMEM((T, R, M, B), BF16),
            pltpu.VMEM((R, T, M, B), BF16),
            pltpu.VMEM((2, T, M, B), BF16),
            pltpu.VMEM((M, B), F32),
            pltpu.VMEM((n_near, B, B), BF16),
            dma,
            dma((2, T)),
            dma((T,)),
            dma((T, R)),
            dma((T, R)),
            dma((T, R)),
            dma((T, R)),
            dma((T,)),
            dma((T,)),
            dma((T, R)),
            dma((T, R)),
            dma((T,)),
            dma((2, T)),
        ],
        compiler_params=pltpu.CompilerParams(
            collective_id=0, has_side_effects=True, vmem_limit_bytes=60 * 1024 * 1024
        ),
        name="operator_twice",
    )(
        tile_col,
        near_col.reshape(n_near),
        sources,
        basis_out.reshape(n_tiles * rank, B),
        basis_in,
        onehot,
        near_blocks.reshape(n_near, B, B),
        jacobi_inverse,
    )


def solution(mesh):
    return jax.shard_map(
        functools.partial(local, mesh.shape["tiles"], mesh.shape["rhs"]),
        mesh=mesh,
        in_specs=(
            P("rhs", ("groups", "tiles", "sub")),
            P(("groups", "tiles", "rhs", "sub"), None, None),
            P(("groups", "tiles", "rhs", "sub"), None, None),
            P(("groups", "tiles", "rhs", "sub")),
            P(("groups", "tiles", "rhs", "sub")),
            P(("groups", "tiles", "rhs", "sub")),
            P(("groups", "tiles", "sub"), None, None, None),
            P(("groups", "tiles", "sub"), None),
            P(("groups", "tiles", "sub"), None, None),
        ),
        out_specs=(P("rhs", ("groups", "tiles", "sub")), P("rhs", ("groups", "tiles", "sub"))),
        check_vma=False,
    )
```

time: 234 us -> 88.5 us (0.38)
  waiting for transfers between devices: 150 us -> 0 us
  Pallas kernels: 0 us -> 83.1 us
  matrix products: 41.5 us -> 0 us
  local copies, waits for them, and re-layouts: 20.9 us -> 3.21 us
  between operations: 14.9 us -> 0.64 us
  blocking collectives: 5.19 us -> 0 us
    all_gather x4 -> x0, waiting for transfers between devices: 88.2 us -> none  [the longest x2 35 us: apply_operator(): lax.all_gather(vector, ('tiles', 'sub'), axis=1, tiled=True)]
    pallas_call x0 -> x1, Pallas kernels: none -> 83.1 us  [local(): pl.pallas_call(functools.partial(kernel, T, R), out_shape=(out, out), in_...]
    reduce_scatter x2 -> x0, waiting for transfers between devices: 60.7 us -> none  [apply_operator(): lax.psum_scatter(far_field.astype(jnp.bfloat16), ('tiles', 'sub'), scatte...]
    dot_general x10 -> x0, matrix products: 41.5 us -> none  [the longest x2 14.4 us: tile_terms(): jnp.einsum('ctr,trp->ctp', coefficients, basis_out, preferred_element_typ...]
    gather x4 -> x0, local copies, waits for them, and re-layouts: 9.13 us -> none  [the longest x2 6.43 us: tile_terms(): picked = jnp.take(gathered, tile_col, axis=1)]
    unnamed x22 -> x2, local copies, waits for them, and re-layouts: 9.77 us -> 3.14 us
    unnamed x1 -> x0, blocking collectives: 5.19 us -> none
  transfers between devices with their start and end apart: 6 -> 0, of which waited for: 6 -> 0; matrix products, arithmetic and copies ran while one was open for 5% -> 0% of each run, Pallas kernels for 0% -> 0%
where the time goes in v1:
time: 88.5 us; the launch traced here: 88.3 us
  Pallas kernels  83.1 us (94%)
  local copies, waits for them, and re-layouts  3.21 us (4%)
  other arithmetic  1.38 us (2%)
    pallas_call x1, Pallas kernels, local(): pl.pallas_call(functools.partial(kernel, T, R), out_shape=(out, out), in_...  83.1 us
    unnamed x2, local copies, waits for them, and re-layouts  3.14 us

profile of v1, /device:TPU:0, one launch (start us, length us, event | category | flops | bytes accessed | tf_op | source)
XLA Modules:
  0.0 88.3 jit_solution(5648098988096900878)
XLA Ops:
  0.6 0.7 fusion
  1.4 0.1 select_n.12
  1.4 0.6 compare_convert_fusion.onehot
  2.1 83.1 %operator_twice.1 = (bf16[128,512]{1,0:T(8,128)(2,1)}, bf16[128,512]{1,0:T(8,128)(2,1)}) custom-call(s32[12]{0:T(128)} %tile_col.1, s32[16]{0:T(128)} %bitcast.5, bf16[128,512]{1,0:T(8,128)(2,1)} %src.1, bf16[768,512]{1,0:T(8,128)(2,1)} %bitcast.4, bf16[12,64,512]{2,1,0:T(8,128)(2,1)} %basis_in.1, f32[8,1,768]{2,1,0:T(1,128)} %compare_convert_fusion.onehot, ...), custom_call_target="tpu_custom_call" | custom-call | tf_op jit(solution)/shard_map/operator_twice/pallas_call | solution.py:367
  85.2 1.6 %copy.13 = bf16[128,512]{1,0:T(8,128)(2,1)} copy(bf16[128,512]{1,0:T(8,128)(2,1)} %get-tuple-element.4) | data formatting | bytes 262144
  86.7 1.6 %copy.14 = bf16[128,512]{1,0:T(8,128)(2,1)} copy(bf16[128,512]{1,0:T(8,128)(2,1)} %get-tuple-element.5) | data formatting | bytes 262144

commit v2 on v1

v2 whole, which is shorter than its diff:
```python
import functools

import jax
import jax.numpy as jnp
from jax import lax
from jax.experimental import pallas as pl
from jax.experimental.pallas import tpu as pltpu
from jax.sharding import PartitionSpec as P

MESH = pl.DeviceIdType.MESH
F32 = jnp.float32
BF16 = jnp.bfloat16
NT = (((1,), (1,)), ((), ()))


def dot_nt(a, b):
    return lax.dot_general(a, b, NT, preferred_element_type=F32)


def kernel(
    T,
    R,
    C,
    tile_rank,
    tile_row,
    tile_col,
    near_col,
    src,
    basis_out,
    basis_in,
    near_hbm,
    jacobi,
    out0,
    out1,
    v0,
    v1,
    coef,
    rows,
    fa,
    fd,
    fx,
    fz,
    nacc,
    near,
    near_sem,
    vz_send,
    vz_recv,
    vx_send,
    vx_recv,
    vd_send,
    vd_recv,
    fd_send,
    fd_recv,
    fx_send,
    fx_recv,
    fz_send,
    fz_recv,
):
    t = lax.axis_index("tiles")
    r = lax.axis_index("rhs")
    s = lax.axis_index("sub")
    M, B = src.shape
    n_tiles, rank, _ = basis_in.shape
    n_near = near_hbm.shape[0]
    has_left, has_right = t > 0, t < T - 1
    sibling = {"sub": 1 - s}
    partners = [lax.rem(r + k, R) for k in range(1, R)]

    def copy(src_ref, dst_ref, send, recv, device):
        return pltpu.make_async_remote_copy(
            src_ref=src_ref,
            dst_ref=dst_ref,
            send_sem=send,
            recv_sem=recv,
            device_id=device,
            device_id_type=MESH,
        )

    near_copy = pltpu.make_async_copy(near_hbm, near, near_sem)

    barrier = pltpu.get_barrier_semaphore()

    @pl.when(has_left)
    def _():
        pl.semaphore_signal(barrier, inc=1, device_id={"tiles": t - 1}, device_id_type=MESH)

    @pl.when(has_right)
    def _():
        pl.semaphore_signal(barrier, inc=1, device_id={"tiles": t + 1}, device_id_type=MESH)

    for q in partners:
        pl.semaphore_signal(barrier, inc=1, device_id={"rhs": q}, device_id_type=MESH)
    pl.semaphore_signal(barrier, inc=1, device_id=sibling, device_id_type=MESH)

    near_copy.start()
    lane = lax.broadcasted_iota(jnp.int32, (1, 2 * rank), 1)
    first = lane < rank
    for k in range(0, n_tiles, 2):
        row = jnp.where(first, tile_row[k], tile_row[k + 1])
        top = jnp.where(first, tile_rank[k], tile_rank[k + 1] + rank)
        rows[:, k * rank : (k + 2) * rank] = jnp.where(lane < top, row, -1)

    neighbours = (t + T - 1) // T + (2 * T - 2 - t) // T
    pl.semaphore_wait(barrier, R + neighbours)

    m = M // C

    def part(c):
        return pl.ds(c * m, m)

    class Gather:
        def __init__(self, v):
            self.v = v

        def z(self, tt, side, c):
            ref = self.v.at[tt * 2 + s, r, part(c)]
            return copy(
                ref, ref, vz_send.at[side, tt, c], vz_recv.at[tt, c], {"tiles": t + 2 * side - 1}
            )

        def x(self, tt, q, c):
            ref = self.v.at[tt * 2 + s, r, part(c)]
            return copy(ref, ref, vx_send.at[tt, q, c], vx_recv.at[tt, r, c], {"rhs": q})

        def x_arrival(self, tt, q, c):
            ref = self.v.at[tt * 2 + s, q, part(c)]
            return copy(ref, ref, vx_send.at[tt, q, c], vx_recv.at[tt, q, c], {"rhs": q})

        def d(self, tt, q, core):
            ref = self.v.at[tt * 2 + core, q]
            return copy(ref, ref, vd_send.at[tt, q], vd_recv.at[tt, q], sibling)

        def pass_on(self, tt):
            for q in partners:
                for c in range(C):
                    self.x_arrival(tt, q, c).wait_recv()
                self.d(tt, q, s).start()

        def begin(self):
            for c in range(C):

                @pl.when(has_left)
                def _():
                    self.z(t, 0, c).start()

                @pl.when(has_right)
                def _():
                    self.z(t, 1, c).start()

                for q in partners:
                    self.x(t, q, c).start()
            self.d(t, r, s).start()

        def forward(self, tt, side, c, onward):
            self.z(tt, side, c).wait_recv()

            @pl.when(onward)
            def _():
                self.z(tt, side, c).start()

            for q in partners:
                self.x(tt, q, c).start()
            if c == C - 1:
                self.d(tt, r, s).start()

        def run(self):
            for d in range(1, T + 1):
                for c in range(C if d < T else 0):

                    @pl.when(t - d >= 0)
                    def _():
                        self.forward(t - d, 1, c, has_right)

                    @pl.when(t + d < T)
                    def _():
                        self.forward(t + d, 0, c, has_left)

                if d == 1:
                    self.pass_on(t)
                else:

                    @pl.when(t - (d - 1) >= 0)
                    def _():
                        self.pass_on(t - (d - 1))

                    @pl.when(t + (d - 1) < T)
                    def _():
                        self.pass_on(t + (d - 1))

            for tt in range(T):
                for q in range(R):
                    self.d(tt, q, 1 - s).wait_recv()

        def finish(self):
            for tt in range(T):
                for c in range(C):

                    @pl.when(has_left & (tt >= t))
                    def _():
                        self.z(tt, 0, c).wait_send()

                    @pl.when(has_right & (tt <= t))
                    def _():
                        self.z(tt, 1, c).wait_send()

                    for q in partners:
                        self.x(tt, q, c).wait_send()
                for q in range(R):
                    self.d(tt, q, s).wait_send()

    def fd_copy(tt):
        return copy(fa.at[tt * 2 + 1 - s], fd.at[tt], fd_send.at[tt], fd_recv.at[tt], sibling)

    def fx_copy(tt, q, c):
        return copy(
            fa.at[tt * 2 + s, q, part(c)],
            fx.at[r, tt, part(c)],
            fx_send.at[tt, q, c],
            fx_recv.at[tt, r, c],
            {"rhs": q},
        )

    def fx_arrival(tt, q, c):
        return copy(
            fa.at[tt * 2 + s, q, part(c)],
            fx.at[q, tt, part(c)],
            fx_send.at[tt, q, c],
            fx_recv.at[tt, q, c],
            {"rhs": q},
        )

    def fz_copy(tt, side, c):
        return copy(
            fa.at[tt * 2 + s, r, part(c)],
            fz.at[side, tt, part(c)],
            fz_send.at[tt, c],
            fz_recv.at[side, tt, c],
            {"tiles": t + 2 * side - 1},
        )

    sign = 2 * ((2 * t) // T) - 1

    def nth(p):
        return (t + sign * (1 + p) + 2 * T) % T

    def far_block(i):
        masked = coef[...] * (rows[...] == i).astype(F32).astype(BF16)
        block = jnp.dot(masked, basis_out[...], preferred_element_type=F32)
        fa[i] = block.astype(BF16).reshape(R, M, B)

    def far_start(v):
        for k in range(0, n_tiles, 2):
            pair = basis_in[k : k + 2].reshape(2 * rank, B)
            picked = [v[tile_col[k + j]].reshape(R * M, B) for j in range(2)]
            both = dot_nt(jnp.concatenate(picked, axis=0), pair)
            coef[:, k * rank : (k + 2) * rank] = jnp.where(
                first, both[: R * M], both[R * M :]
            ).astype(BF16)

        @pl.loop(0, T)
        def _(p):
            tt = nth(p)
            far_block(tt * 2 + 1 - s)
            fd_copy(tt).start()

        @pl.loop(0, T)
        def _(p):
            tt = nth(p)
            far_block(tt * 2 + s)
            fd_copy(tt).wait_recv()
            fa[tt * 2 + s] = (fa[tt * 2 + s].astype(F32) + fd[tt].astype(F32)).astype(BF16)
            for q in partners:
                for c in range(C):
                    fx_copy(tt, q, c).start()

    def near_field(v):
        total = None
        for k in range(n_near):
            term = dot_nt(v[near_col[k], r], near[k])
            if k == 0:
                nacc[...] = term
            else:
                nacc[...] += term

    def far_end():
        def settle(tt, side, c, more):
            here = part(c)
            acc = fa[tt * 2 + s, r, here].astype(F32)
            for q in partners:
                fx_arrival(tt, q, c).wait_recv()
                acc += fx[q, tt, here].astype(F32)
            fa[tt * 2 + s, r, here] = acc.astype(BF16)

            @pl.when(more)
            def _():
                fz_copy(tt, side, c).wait_recv()
                total = fa[tt * 2 + s, r, here].astype(F32) + fz[side, tt, here].astype(F32)
                fa[tt * 2 + s, r, here] = total.astype(BF16)

            fz_copy(tt, side, c).start()

        for d in range(T - 1, 0, -1):
            for c in range(C):

                @pl.when(t + d < T)
                def _():
                    settle(t + d, 1, c, has_left)

                @pl.when(t - d >= 0)
                def _():
                    settle(t - d, 0, c, has_right)

        for c in range(C):
            here = part(c)
            acc = nacc[here] + fa[t * 2 + s, r, here].astype(F32)
            for q in partners:
                fx_arrival(t, q, c).wait_recv()
                acc += fx[q, t, here].astype(F32)
            nacc[here] = acc

        for c in range(C):
            here = part(c)

            @pl.when(has_left)
            def _():
                fz_copy(t, 1, c).wait_recv()
                nacc[here] += fz[1, t, here].astype(F32)

            @pl.when(has_right)
            def _():
                fz_copy(t, 0, c).wait_recv()
                nacc[here] += fz[0, t, here].astype(F32)

    def far_finish():
        for tt in range(T):
            fd_copy(tt).wait_send()
            for c in range(C):
                for q in partners:
                    fx_copy(tt, q, c).wait_send()

                @pl.when(tt > t)
                def _():
                    fz_copy(tt, 1, c).wait_send()

                @pl.when(tt < t)
                def _():
                    fz_copy(tt, 0, c).wait_send()

    one, two = Gather(v0), Gather(v1)
    v0[t * 2 + s, r] = src[...]
    one.begin()
    one.run()
    far_start(v0)
    near_copy.wait()
    near_field(v0)
    far_end()
    result = precondition(nacc[...].astype(BF16), jacobi)
    v1[t * 2 + s, r] = result
    one.finish()
    two.begin()
    out0[...] = result
    two.run()
    far_finish()
    far_start(v1)
    near_field(v1)
    far_end()
    out1[...] = nacc[...].astype(BF16)
    two.finish()
    far_finish()


def precondition(field, jacobi):
    jb = jacobi.shape[1]
    groups = [
        dot_nt(field[:, g * jb : (g + 1) * jb], jacobi[g]).astype(BF16)
        for g in range(jacobi.shape[0])
    ]
    return jnp.concatenate(groups, axis=1)


def last_kernel(first, field, jacobi, out0, out1):
    out0[...] = first[...]
    out1[...] = precondition(field[...], jacobi)


def local(
    T,
    R,
    sources,
    basis_out,
    basis_in,
    tile_rank,
    tile_row,
    tile_col,
    near_blocks,
    near_col,
    jacobi_inverse,
):
    n_tiles, rank, B = basis_in.shape
    M = sources.shape[0]
    NB = 2 * T
    C = 2
    n_near = near_blocks.shape[1]
    vmem = pl.BlockSpec(memory_space=pltpu.VMEM)
    smem = pl.BlockSpec(memory_space=pltpu.SMEM)
    dma = pltpu.SemaphoreType.DMA
    out = jax.ShapeDtypeStruct((M, B), BF16)
    first, field = pl.pallas_call(
        functools.partial(kernel, T, R, C),
        out_shape=(out, out),
        in_specs=[smem] * 4 + [vmem] * 3 + [pl.BlockSpec(memory_space=pl.ANY), vmem],
        out_specs=(vmem, vmem),
        scratch_shapes=[
            pltpu.VMEM((NB, R, M, B), BF16),
            pltpu.VMEM((NB, R, M, B), BF16),
            pltpu.VMEM((R * M, n_tiles * rank), BF16),
            pltpu.VMEM((1, n_tiles * rank), jnp.int32),
            pltpu.VMEM((NB, R, M, B), BF16),
            pltpu.VMEM((T, R, M, B), BF16),
            pltpu.VMEM((R, T, M, B), BF16),
            pltpu.VMEM((2, T, M, B), BF16),
            pltpu.VMEM((M, B), F32),
            pltpu.VMEM((n_near, B, B), BF16),
            dma,
            dma((2, T, C)),
            dma((T, C)),
            dma((T, R, C)),
            dma((T, R, C)),
            dma((T, R)),
            dma((T, R)),
            dma((T,)),
            dma((T,)),
            dma((T, R, C)),
            dma((T, R, C)),
            dma((T, C)),
            dma((2, T, C)),
        ],
        compiler_params=pltpu.CompilerParams(
            collective_id=0, has_side_effects=True, vmem_limit_bytes=60 * 1024 * 1024
        ),
        name="operator_twice",
    )(
        tile_rank,
        tile_row,
        tile_col,
        near_col.reshape(n_near),
        sources,
        basis_out.reshape(n_tiles * rank, B),
        basis_in,
        near_blocks.reshape(n_near, B, B),
        jacobi_inverse,
    )
    return pl.pallas_call(
        last_kernel,
        out_shape=(out, out),
        in_specs=[vmem] * 3,
        out_specs=(vmem, vmem),
        name="last_precondition",
    )(first, field, jacobi_inverse)


def solution(mesh):
    return jax.shard_map(
        functools.partial(local, mesh.shape["tiles"], mesh.shape["rhs"]),
        mesh=mesh,
        in_specs=(
            P("rhs", ("groups", "tiles", "sub")),
            P(("groups", "tiles", "rhs", "sub"), None, None),
            P(("groups", "tiles", "rhs", "sub"), None, None),
            P(("groups", "tiles", "rhs", "sub")),
            P(("groups", "tiles", "rhs", "sub")),
            P(("groups", "tiles", "rhs", "sub")),
            P(("groups", "tiles", "sub"), None, None, None),
            P(("groups", "tiles", "sub"), None),
            P(("groups", "tiles", "sub"), None, None),
        ),
        out_specs=(P("rhs", ("groups", "tiles", "sub")), P("rhs", ("groups", "tiles", "sub"))),
        check_vma=False,
    )
```

time: 88.5 us -> 80 us (0.904)
  Pallas kernels: 83.1 us -> 79.2 us
  local copies, waits for them, and re-layouts: 3.21 us -> 0 us
  other arithmetic: 1.38 us -> 0 us
    pallas_call x1 -> x2, Pallas kernels: 83.1 us -> 79.2 us  [the longest x1 77.3 us: local(): pl.pallas_call(functools.partial(kernel, T, R, C), out_shape=(out, out),...]
    unnamed x2 -> x0, local copies, waits for them, and re-layouts: 3.14 us -> none
where the time goes in v2:
time: 80 us; the launch traced here: 79.9 us
  Pallas kernels  79.2 us (99%)
    pallas_call x1, Pallas kernels, local(): pl.pallas_call(functools.partial(kernel, T, R, C), out_shape=(out, out),...  77.3 us
    pallas_call x1, Pallas kernels, local(): pl.pallas_call(last_kernel, out_shape=(out, out), in_specs=[vmem] * 3, ou...  1.9 us

profile of v2, /device:TPU:0, one launch (start us, length us, event | category | flops | bytes accessed | tf_op | source)
XLA Modules:
  0.0 79.9 jit_solution(11335265342124668540)
XLA Ops:
  0.6 77.3 %operator_twice.1 = (bf16[128,512]{1,0:T(8,128)(2,1)}, bf16[128,512]{1,0:T(8,128)(2,1)}) custom-call(s32[12]{0:T(128)} %tile_rank.1, s32[12]{0:T(128)} %tile_row.1, s32[12]{0:T(128)} %tile_col.1, s32[16]{0:T(128)} %bitcast.5, bf16[128,512]{1,0:T(8,128)(2,1)} %src.1, bf16[768,512]{1,0:T(8,128)(2,1)} %bitcast.4, bf16[12,64,512]{2,1,0:T(8,128)(2,1)} %basis_in.1, ...), custom_call_target="tpu_custom_call" | custom-call | tf_op jit(solution)/shard_map/operator_twice/pallas_call | solution.py:408
  78.0 1.9 %last_precondition.1 = (bf16[128,512]{1,0:T(8,128)(2,1)}, bf16[128,512]{1,0:T(8,128)(2,1)}) custom-call(bf16[128,512]{1,0:T(8,128)(2,1)} %get-tuple-element.4.first, bf16[128,512]{1,0:T(8,128)(2,1)} %get-tuple-element.5.field, bf16[4,128,128]{2,1,0:T(8,128)(2,1)} %jacobi.3), custom_call_target="tpu_custom_call" | custom-call | tf_op jit(solution)/shard_map/last_precondition/pallas_call | solution.py:453

commit v3 on v2

--- a/solution.py
+++ b/solution.py
@@ -399,7 +399,7 @@
     n_tiles, rank, B = basis_in.shape
     M = sources.shape[0]
     NB = 2 * T
-    C = 2
+    C = max(1, M // 32)
     n_near = near_blocks.shape[1]
     vmem = pl.BlockSpec(memory_space=pltpu.VMEM)
     smem = pl.BlockSpec(memory_space=pltpu.SMEM)

time: 80 us -> 77.5 us (0.969)
  Pallas kernels: 79.2 us -> 76.7 us
    pallas_call x1, Pallas kernels: 77.3 us -> 74.8 us  [local(): pl.pallas_call(functools.partial(kernel, T, R, C), out_shape=(out, out),...]
where the time goes in v3:
time: 77.5 us; the launch traced here: 77.3 us
  Pallas kernels  76.7 us (99%)
    pallas_call x1, Pallas kernels, local(): pl.pallas_call(functools.partial(kernel, T, R, C), out_shape=(out, out),...  74.8 us
    pallas_call x1, Pallas kernels, local(): pl.pallas_call(last_kernel, out_shape=(out, out), in_specs=[vmem] * 3, ou...  1.9 us

profile of v3, /device:TPU:0, one launch (start us, length us, event | category | flops | bytes accessed | tf_op | source)
XLA Modules:
  0.0 77.3 jit_solution(9420307242582729563)
XLA Ops:
  0.6 74.8 %operator_twice.1 = (bf16[128,512]{1,0:T(8,128)(2,1)}, bf16[128,512]{1,0:T(8,128)(2,1)}) custom-call(s32[12]{0:T(128)} %tile_rank.1, s32[12]{0:T(128)} %tile_row.1, s32[12]{0:T(128)} %tile_col.1, s32[16]{0:T(128)} %bitcast.5, bf16[128,512]{1,0:T(8,128)(2,1)} %src.1, bf16[768,512]{1,0:T(8,128)(2,1)} %bitcast.4, bf16[12,64,512]{2,1,0:T(8,128)(2,1)} %basis_in.1, ...), custom_call_target="tpu_custom_call" | custom-call | tf_op jit(solution)/shard_map/operator_twice/pallas_call | solution.py:408
  75.4 1.9 %last_precondition.1 = (bf16[128,512]{1,0:T(8,128)(2,1)}, bf16[128,512]{1,0:T(8,128)(2,1)}) custom-call(bf16[128,512]{1,0:T(8,128)(2,1)} %get-tuple-element.4.first, bf16[128,512]{1,0:T(8,128)(2,1)} %get-tuple-element.5.field, bf16[4,128,128]{2,1,0:T(8,128)(2,1)} %jacobi.3), custom_call_target="tpu_custom_call" | custom-call | tf_op jit(solution)/shard_map/last_precondition/pallas_call | solution.py:453
